TPU v7x, 512 devices: a whole 4x8x8 slice. The times are simulated.
512 devices in a mesh: delay: 16 (over y, core), row: 32 (over z, x).
Axes of the slice: x: 4, y: 8, z: 8, core: 2. Of those that a mesh axis runs over, the one named last changes fastest.
Arguments:
- incident: bfloat16 [64, 4096], P(None, 'row'), may hold values from -12 to 12
- onset: int32 [64], replicated, may hold values from 0 to 2
- beta: float32 [4096], P('delay'), may hold values from 0.05 to 0.5
- inverse_block: bfloat16 [4096, 4096], P('row', 'delay'), may hold values from -0.0625 to 0.0625
- delay_blocks: bfloat16 [16, 4096, 4096], P('delay', None, 'row'), may hold values from -0.09375 to 0.09375
- history_sum: float32 [16, 64, 4096], P('delay', None, 'row'), may hold values from -12 to 12
Outputs:
- currents: bfloat16 [3, 64, 4096], P(None, None, 'delay')
- carried: float32 [16, 64, 4096], P('delay', None, 'row')
All inputs are finite; a program needn't handle non-finite values.
Results may differ from a plain program's by a relative error of at most 0.0056.
Values may be sent and summed in bfloat16 or wider, within the bound.
A program may use at most 64 MiB of HBM per device.

v0:
```python
import jax
import jax.numpy as jnp
from jax import lax
from jax.sharding import PartitionSpec as P

STEPS = 3


def broadcast(value, axis, root):
    return lax.dynamic_index_in_dim(lax.all_gather(value, axis), root, 0, keepdims=False)


def in_blocks(value, dim, devices):
    dims = value.shape
    blocks = value.reshape(*dims[:dim], devices, dims[dim] // devices, *dims[dim + 1 :])
    return jnp.moveaxis(blocks, dim, 0)


def sent_and_summed(value, axis, dim):
    devices = lax.axis_size(axis)
    blocks = lax.all_to_all(in_blocks(value, dim, devices), axis, 0, 0, tiled=True)
    return jnp.sum(blocks, axis=0)


def copy_for_each(value, axis):
    copies = jnp.broadcast_to(value, (lax.axis_size(axis), *value.shape))
    return lax.all_to_all(copies, axis, split_axis=0, concat_axis=0, tiled=True)


def joined_along(blocks, dim):
    blocks = jnp.moveaxis(blocks, 0, dim)
    dims = blocks.shape
    return blocks.reshape(*dims[:dim], dims[dim] * dims[dim + 1], *dims[dim + 2 :])


def gathered_copies(value, axis, dim):
    blocks = copy_for_each(value, axis)
    return joined_along(blocks, dim)


def passed_along(value, axis, by):
    devices = lax.axis_size(axis)
    pairs = [(i, i + by) for i in range(devices) if 0 <= i + by < devices]
    return lax.ppermute(value, axis, pairs)


def per_device(incident, onset, beta, inverse_block, delay_blocks, history_sum):
    future = history_sum[0]
    matrix = delay_blocks[0]
    incident_wide = incident.astype(jnp.float32)
    outputs = []
    for step_index in range(STEPS):
        offset_time = (step_index - onset).astype(jnp.float32)
        envelope = jnp.where(offset_time >= 0.0, jnp.exp(-((offset_time - 1.0) ** 2) / 4.0), 0.0)
        residual = (incident_wide * envelope[:, None] - future).astype(jnp.bfloat16)
        residual = broadcast(residual, "delay", 0)
        partial_sum = jnp.dot(residual, inverse_block, preferred_element_type=jnp.float32)
        solved = sent_and_summed(partial_sum, "row", 0)
        current = (solved / (1.0 + beta[None, :] * solved * solved)).astype(jnp.bfloat16)
        own_block = gathered_copies(current, "row", 0)
        gathered = lax.all_gather(own_block, "delay", axis=1, tiled=True)
        outputs.append(own_block)
        passed = passed_along(future, "delay", -1)
        future = passed + jnp.dot(gathered, matrix, preferred_element_type=jnp.float32)
    return (jnp.stack(outputs), future[None])


def solution(mesh):
    placed = (
        P(None, "row"),
        P(),
        P("delay"),
        P("row", "delay"),
        P("delay", None, "row"),
        P("delay", None, "row"),
    )
    return jax.shard_map(
        per_device,
        mesh=mesh,
        in_specs=placed,
        out_specs=(P(None, None, "delay"), P("delay", None, "row")),
        check_vma=False,
    )
```

profile of v0, /device:TPU:1, one launch (start us, length us, event | category | flops | bytes accessed | tf_op | source)
XLA Modules:
  0.0 199.1 jit_solution(9493592428893358727)
XLA Ops:
  0.6 0.0 copy-start
  0.6 0.8 compare_select_fusion.1
  1.4 0.9 fusion.12
  2.3 0.0 copy-start.1
  2.3 21.7 %all-gather = bf16[1024,128]{1,0:T(8,128)(2,1)S(1)} all-gather(bf16[64,128]{1,0:T(8,128)(2,1)S(1)} %fusion.12), channel_id=2, replica_groups=mesh['delay'=16,'row'=32] {'delay'}, dimensions={0}, use_global_device_ids=true | all-gather | bytes 278528 | tf_op jit(solution)/shard_map/all_gather | solution.py:10
  24.0 0.0 copy-done.1
  24.0 0.1 fusion.9
  24.1 0.1 copy.14
  24.2 19.6 %all_to_all.30 = f32[32,2,256]{2,1,0:T(2,128)S(1)} all-to-all(f32[32,2,256]{2,1,0:T(2,128)S(1)} %copy.14), channel_id=1, replica_groups=mesh['delay'=16,'row'=32] {'row'}, dimensions={0} | all-to-all | bytes 131072 | tf_op jit(solution)/shard_map/all_to_all | solution.py:21
  43.8 0.0 copy-start.4
  43.8 0.6 copy-done.4
  44.5 0.6 broadcast_in_dim.22
  45.1 0.0 copy-start.3
  45.1 4.0 %all-to-all-start.1 = ((bf16[32,2,256]{2,1,0:T(2,128)(2,1)}), bf16[32,2,256]{2,1,0:T(2,128)(2,1)S(1)}, u32[]{:S(2)}, u32[]{:S(2)}) async-start(bf16[32,2,256]{2,1,0:T(2,128)(2,1)} %broadcast_in_dim.22), calls=%async_computation.1 | async-start | bytes 65536 | tf_op jit(solution)/shard_map/all_to_all | solution.py:27
  49.1 0.0 copy-done.3
  49.1 3.5 %collective-permute-start = (f32[64,128]{1,0:T(8,128)S(1)}, f32[64,128]{1,0:T(8,128)S(1)}, u32[]{:S(2)}, u32[]{:S(2)}) collective-permute-start(f32[64,128]{1,0:T(8,128)S(1)} %bitcast.29), channel_id=1, source_target_pairs={{32,0},{64,32},{96,64},{128,96},{160,128},{192,160},{224,192},{256... | collective-permute-start | bytes 98312 | tf_op jit(solution)/shard_map/ppermute | solution.py:44
  52.6 5.1 %all-to-all-done.1 = bf16[32,2,256]{2,1,0:T(2,128)(2,1)S(1)} async-done(((bf16[32,2,256]{2,1,0:T(2,128)(2,1)}), bf16[32,2,256]{2,1,0:T(2,128)(2,1)S(1)}, u32[]{:S(2)}, u32[]{:S(2)}) %all-to-all-start.1) | async-done | bytes 32800 | tf_op jit(solution)/shard_map/all_to_all | solution.py:27
  57.7 0.0 copy-start.2
  57.8 18.9 %all_gather.29 = bf16[64,4096]{1,0:T(8,128)(2,1)S(1)} all-gather(bf16[64,256]{1,0:T(8,128)(2,1)S(1)} %reshape.26), channel_id=1, replica_groups=mesh['delay'=16,'row'=32] {'delay'}, dimensions={1}, use_global_device_ids=true | all-gather | bytes 557056 | tf_op jit(solution)/shard_map/all_gather | solution.py:61
  76.7 0.0 collective-permute-done
  76.7 0.0 copy-done
  76.7 0.0 copy-done.2
  76.7 0.3 fusion.14
  77.0 16.0 %all-gather.1 = bf16[1024,128]{1,0:T(8,128)(2,1)S(1)} all-gather(bf16[64,128]{1,0:T(8,128)(2,1)S(1)} %get-tuple-element.7), channel_id=3, replica_groups=mesh['delay'=16,'row'=32] {'delay'}, dimensions={0}, use_global_device_ids=true | all-gather | bytes 278528 | tf_op jit(solution)/shard_map/all_gather | solution.py:10
  93.1 0.1 fusion.7
  93.2 0.1 copy.16
  93.3 11.8 %all_to_all.31 = f32[32,2,256]{2,1,0:T(2,128)S(1)} all-to-all(f32[32,2,256]{2,1,0:T(2,128)S(1)} %copy.16), channel_id=1, replica_groups=mesh['delay'=16,'row'=32] {'row'}, dimensions={0} | all-to-all | bytes 131072 | tf_op jit(solution)/shard_map/all_to_all | solution.py:21
  105.2 0.6 broadcast_in_dim.23
  105.8 3.9 %all-to-all-start.3 = ((bf16[32,2,256]{2,1,0:T(2,128)(2,1)}), bf16[32,2,256]{2,1,0:T(2,128)(2,1)S(1)}, u32[]{:S(2)}, u32[]{:S(2)}) async-start(bf16[32,2,256]{2,1,0:T(2,128)(2,1)} %broadcast_in_dim.23), calls=%async_computation.3 | async-start | bytes 65536 | tf_op jit(solution)/shard_map/all_to_all | solution.py:27
  109.7 3.3 %collective-permute-start.1 = (f32[64,128]{1,0:T(8,128)S(1)}, f32[64,128]{1,0:T(8,128)S(1)}, u32[]{:S(2)}, u32[]{:S(2)}) collective-permute-start(f32[64,128]{1,0:T(8,128)S(1)} %get-tuple-element.8), channel_id=1, source_target_pairs={{32,0},{64,32},{96,64},{128,96},{160,128},{192,160},{224,192},{256... | collective-permute-start | bytes 98312 | tf_op jit(solution)/shard_map/ppermute | solution.py:44
  113.0 5.3 %all-to-all-done.3 = bf16[32,2,256]{2,1,0:T(2,128)(2,1)S(1)} async-done(((bf16[32,2,256]{2,1,0:T(2,128)(2,1)}), bf16[32,2,256]{2,1,0:T(2,128)(2,1)S(1)}, u32[]{:S(2)}, u32[]{:S(2)}) %all-to-all-start.3) | async-done | bytes 32800 | tf_op jit(solution)/shard_map/all_to_all | solution.py:27
  118.3 18.7 %all_gather.32 = bf16[64,4096]{1,0:T(8,128)(2,1)S(1)} all-gather(bf16[64,256]{1,0:T(8,128)(2,1)S(1)} %reshape.27), channel_id=1, replica_groups=mesh['delay'=16,'row'=32] {'delay'}, dimensions={1}, use_global_device_ids=true | all-gather | bytes 557056 | tf_op jit(solution)/shard_map/all_gather | solution.py:61
  137.0 0.3 fusion.2
  137.4 0.0 collective-permute-done.1
  137.4 0.1 fusion.16
  137.5 16.0 %all-gather.2 = bf16[1024,128]{1,0:T(8,128)(2,1)S(1)} all-gather(bf16[64,128]{1,0:T(8,128)(2,1)S(1)} %get-tuple-element.2), channel_id=4, replica_groups=mesh['delay'=16,'row'=32] {'delay'}, dimensions={0}, use_global_device_ids=true | all-gather | bytes 278528 | tf_op jit(solution)/shard_map/all_gather | solution.py:10
  153.5 0.1 fusion.5
  153.6 0.1 copy.18
  153.7 11.8 %all_to_all.32 = f32[32,2,256]{2,1,0:T(2,128)S(1)} all-to-all(f32[32,2,256]{2,1,0:T(2,128)S(1)} %copy.18), channel_id=1, replica_groups=mesh['delay'=16,'row'=32] {'row'}, dimensions={0} | all-to-all | bytes 131072 | tf_op jit(solution)/shard_map/all_to_all | solution.py:21
  165.6 0.6 broadcast_in_dim.24
  166.2 3.9 %all-to-all-start.5 = ((bf16[32,2,256]{2,1,0:T(2,128)(2,1)}), bf16[32,2,256]{2,1,0:T(2,128)(2,1)S(1)}, u32[]{:S(2)}, u32[]{:S(2)}) async-start(bf16[32,2,256]{2,1,0:T(2,128)(2,1)} %broadcast_in_dim.24), calls=%async_computation.5 | async-start | bytes 65536 | tf_op jit(solution)/shard_map/all_to_all | solution.py:27
  170.1 3.3 %collective-permute-start.2 = (f32[64,128]{1,0:T(8,128)S(1)}, f32[64,128]{1,0:T(8,128)S(1)}, u32[]{:S(2)}, u32[]{:S(2)}) collective-permute-start(f32[64,128]{1,0:T(8,128)S(1)} %get-tuple-element.3), channel_id=1, source_target_pairs={{32,0},{64,32},{96,64},{128,96},{160,128},{192,160},{224,192},{256... | collective-permute-start | bytes 98312 | tf_op jit(solution)/shard_map/ppermute | solution.py:44
  173.4 5.3 %all-to-all-done.5 = bf16[32,2,256]{2,1,0:T(2,128)(2,1)S(1)} async-done(((bf16[32,2,256]{2,1,0:T(2,128)(2,1)}), bf16[32,2,256]{2,1,0:T(2,128)(2,1)S(1)}, u32[]{:S(2)}, u32[]{:S(2)}) %all-to-all-start.5) | async-done | bytes 32800 | tf_op jit(solution)/shard_map/all_to_all | solution.py:27
  178.7 18.7 %all_gather.35 = bf16[64,4096]{1,0:T(8,128)(2,1)S(1)} all-gather(bf16[64,256]{1,0:T(8,128)(2,1)S(1)} %reshape.28), channel_id=1, replica_groups=mesh['delay'=16,'row'=32] {'delay'}, dimensions={1}, use_global_device_ids=true | all-gather | bytes 557056 | tf_op jit(solution)/shard_map/all_gather | solution.py:61
  197.5 0.3 fusion
  197.8 0.7 pad_maximum_fusion
  198.5 0.0 collective-permute-done.2
  198.5 0.6 add_bitcast_fusion
  (15 shorter events, 0.3 us)
Async XLA Ops:
  0.6 76.0 %copy-start = (bf16[1,4096,128]{2,1,0:T(8,128)(2,1)S(1)}, bf16[1,4096,128]{2,1,0:T(8,128)(2,1)}, u32[]{:S(2)}) copy-start(bf16[1,4096,128]{2,1,0:T(8,128)(2,1)} %param.10) | copy-start | bytes 3145732
  2.3 21.7 %copy-start.1 = (bf16[128,256]{1,0:T(8,128)(2,1)S(1)}, bf16[128,256]{1,0:T(8,128)(2,1)}, u32[]{:S(2)}) copy-start(bf16[128,256]{1,0:T(8,128)(2,1)} %param.9) | copy-start | bytes 196612
  43.8 0.7 copy-start.4
  45.1 4.0 %copy-start.3 = (f32[1,64,128]{2,1,0:T(8,128)S(1)}, f32[1,64,128]{2,1,0:T(8,128)}, u32[]{:S(2)}) copy-start(f32[1,64,128]{2,1,0:T(8,128)} %param.11) | copy-start | bytes 98308
  45.1 12.6 %all-to-all-start.1 = ((bf16[32,2,256]{2,1,0:T(2,128)(2,1)}), bf16[32,2,256]{2,1,0:T(2,128)(2,1)S(1)}, u32[]{:S(2)}, u32[]{:S(2)}) async-start(bf16[32,2,256]{2,1,0:T(2,128)(2,1)} %broadcast_in_dim.22), calls=%async_computation.1 | async-start | bytes 65536 | tf_op jit(solution)/shard_map/all_to_all | solution.py:27
  49.1 27.6 %collective-permute-start = (f32[64,128]{1,0:T(8,128)S(1)}, f32[64,128]{1,0:T(8,128)S(1)}, u32[]{:S(2)}, u32[]{:S(2)}) collective-permute-start(f32[64,128]{1,0:T(8,128)S(1)} %bitcast.29), channel_id=1, source_target_pairs={{32,0},{64,32},{96,64},{128,96},{160,128},{192,160},{224,192},{256... | collective-permute-start | bytes 98312 | tf_op jit(solution)/shard_map/ppermute | solution.py:44
  57.7 18.9 %copy-start.2 = (bf16[64,128]{1,0:T(8,128)(2,1)S(1)}, bf16[64,128]{1,0:T(8,128)(2,1)}, u32[]{:S(2)}) copy-start(bf16[64,128]{1,0:T(8,128)(2,1)} %param.6) | copy-start | bytes 49156
  105.8 12.5 %all-to-all-start.3 = ((bf16[32,2,256]{2,1,0:T(2,128)(2,1)}), bf16[32,2,256]{2,1,0:T(2,128)(2,1)S(1)}, u32[]{:S(2)}, u32[]{:S(2)}) async-start(bf16[32,2,256]{2,1,0:T(2,128)(2,1)} %broadcast_in_dim.23), calls=%async_computation.3 | async-start | bytes 65536 | tf_op jit(solution)/shard_map/all_to_all | solution.py:27
  109.7 27.7 %collective-permute-start.1 = (f32[64,128]{1,0:T(8,128)S(1)}, f32[64,128]{1,0:T(8,128)S(1)}, u32[]{:S(2)}, u32[]{:S(2)}) collective-permute-start(f32[64,128]{1,0:T(8,128)S(1)} %get-tuple-element.8), channel_id=1, source_target_pairs={{32,0},{64,32},{96,64},{128,96},{160,128},{192,160},{224,192},{256... | collective-permute-start | bytes 98312 | tf_op jit(solution)/shard_map/ppermute | solution.py:44
  166.2 12.5 %all-to-all-start.5 = ((bf16[32,2,256]{2,1,0:T(2,128)(2,1)}), bf16[32,2,256]{2,1,0:T(2,128)(2,1)S(1)}, u32[]{:S(2)}, u32[]{:S(2)}) async-start(bf16[32,2,256]{2,1,0:T(2,128)(2,1)} %broadcast_in_dim.24), calls=%async_computation.5 | async-start | bytes 65536 | tf_op jit(solution)/shard_map/all_to_all | solution.py:27
  170.1 28.4 %collective-permute-start.2 = (f32[64,128]{1,0:T(8,128)S(1)}, f32[64,128]{1,0:T(8,128)S(1)}, u32[]{:S(2)}, u32[]{:S(2)}) collective-permute-start(f32[64,128]{1,0:T(8,128)S(1)} %get-tuple-element.3), channel_id=1, source_target_pairs={{32,0},{64,32},{96,64},{128,96},{160,128},{192,160},{224,192},{256... | collective-permute-start | bytes 98312 | tf_op jit(solution)/shard_map/ppermute | solution.py:44
where the time goes:
time: 200 us; the launch traced here: 199 us
  blocking collectives  153 us (76%)
  starting transfers between devices  21.8 us (11%)
  waiting for transfers between devices  15.7 us (8%)
  other arithmetic  3.13 us (2%)
  local copies, waits for them, and re-layouts  2.87 us (1%)
    all_gather x3, blocking collectives, per_device(): gathered = lax.all_gather(own_block, 'delay', axis=1, tiled=True)  56.4 us
    all_gather x3, blocking collectives, broadcast(): lax.all_gather(value, axis)  53.8 us
    all_to_all x3, blocking collectives, sent_and_summed(): lax.all_to_all(in_blocks(value, dim, devices), axis, 0, 0, tiled=True)  43.3 us
    all_to_all x3, waiting for transfers between devices, copy_for_each(): return lax.all_to_all(copies, axis, split_axis=0, concat_axis=0, tiled=True)  15.7 us
    all_to_all x3, starting transfers between devices, copy_for_each(): return lax.all_to_all(copies, axis, split_axis=0, concat_axis=0, tiled=True)  11.7 us
    ppermute x3, starting transfers between devices, passed_along(): return lax.ppermute(value, axis, pairs)  10.1 us
  transfers between devices with their start and end apart: 6, of which 3 were waited for; matrix products, arithmetic and copies ran while one was open for 1% of the time, Pallas kernels for 0%

commit v1 on v0

--- a/solution.py
+++ b/solution.py
@@ -4,6 +4,27 @@
 from jax.sharding import PartitionSpec as P
 
 STEPS = 3
+
+
+def collect(value, axis, dim):
+    size, index, width = (lax.axis_size(axis), lax.axis_index(axis), value.shape[dim])
+    forward = [(i, (i + 1) % size) for i in range(size)]
+    left = [(i, (i - 1) % size) for i in range(size)]
+    result = jnp.zeros((*value.shape[:dim], size * width, *value.shape[dim + 1 :]), value.dtype)
+    result = lax.dynamic_update_slice_in_dim(result, value, index * width, axis=dim)
+    from_left = from_right = value
+    middle = size // 2
+    for step in range(1, middle + 1):
+        from_left = lax.ppermute(from_left, axis, forward)
+        result = lax.dynamic_update_slice_in_dim(
+            result, from_left, (index - step) % size * width, axis=dim
+        )
+        if step < size - middle:
+            from_right = lax.ppermute(from_right, axis, left)
+            result = lax.dynamic_update_slice_in_dim(
+                result, from_right, (index + step) % size * width, axis=dim
+            )
+    return result
 
 
 def broadcast(value, axis, root):
@@ -58,7 +79,7 @@
         solved = sent_and_summed(partial_sum, "row", 0)
         current = (solved / (1.0 + beta[None, :] * solved * solved)).astype(jnp.bfloat16)
         own_block = gathered_copies(current, "row", 0)
-        gathered = lax.all_gather(own_block, "delay", axis=1, tiled=True)
+        gathered = collect(own_block, "delay", 1)
         outputs.append(own_block)
         passed = passed_along(future, "delay", -1)
         future = passed + jnp.dot(gathered, matrix, preferred_element_type=jnp.float32)

time: 200 us -> 255 us (1.27)
  starting transfers between devices: 21.8 us -> 94.7 us
  blocking collectives: 153 us -> 102 us
  waiting for transfers between devices: 15.7 us -> 46.9 us
    ppermute x0 -> x45, starting transfers between devices: none -> 72.9 us  [the longest x21 44.6 us: collect(): from_right = lax.ppermute(from_right, axis, left)]
    all_gather x3 -> x0, blocking collectives: 56.4 us -> none  [per_device(): gathered = lax.all_gather(own_block, 'delay', axis=1, tiled=True)]
    ppermute x0 -> x45, waiting for transfers between devices: none -> 31.4 us  [the longest x24 27.7 us: collect(): from_left = lax.ppermute(from_left, axis, forward)]
    all_gather x3, blocking collectives: 53.8 us -> 58.8 us  [broadcast(): lax.all_gather(value, axis)]
  transfers between devices with their start and end apart: 6 -> 51, of which waited for: 3 -> 44; matrix products, arithmetic and copies ran while one was open for 1% -> 0% of each run, Pallas kernels for 0% -> 0%
where the time goes in v1:
time: 255 us; the launch traced here: 253 us
  blocking collectives  102 us (40%)
  starting transfers between devices  94.7 us (37%)
  waiting for transfers between devices  46.9 us (18%)
  local copies, waits for them, and re-layouts  3.2 us (1%)
    all_gather x3, blocking collectives, broadcast(): lax.all_gather(value, axis)  58.8 us
    ppermute x21, starting transfers between devices, collect(): from_right = lax.ppermute(from_right, axis, left)  44.6 us
    all_to_all x3, blocking collectives, sent_and_summed(): lax.all_to_all(in_blocks(value, dim, devices), axis, 0, 0, tiled=True)  43.3 us
    ppermute x24, starting transfers between devices, collect(): from_left = lax.ppermute(from_left, axis, forward)  28.3 us
    ppermute x24, waiting for transfers between devices, collect(): from_left = lax.ppermute(from_left, axis, forward)  27.7 us
    all_to_all x3, waiting for transfers between devices, copy_for_each(): return lax.all_to_all(copies, axis, split_axis=0, concat_axis=0, tiled=True)  15.5 us
    all_to_all x3, starting transfers between devices, copy_for_each(): return lax.all_to_all(copies, axis, split_axis=0, concat_axis=0, tiled=True)  11.7 us
    ppermute x3, starting transfers between devices, passed_along(): return lax.ppermute(value, axis, pairs)  10.1 us
  transfers between devices with their start and end apart: 51, of which 44 were waited for; matrix products, arithmetic and copies ran while one was open for 0% of the time, Pallas kernels for 0%

profile of v1, /device:TPU:1, one launch (start us, length us, event | category | flops | bytes accessed | tf_op | source)
XLA Modules:
  0.0 252.5 jit_solution(7011252682303449512)
XLA Ops:
  0.6 0.8 compare_select_fusion
  1.4 0.9 fusion.11
  2.3 21.7 %all-gather = bf16[1024,128]{1,0:T(8,128)(2,1)S(1)} all-gather(bf16[64,128]{1,0:T(8,128)(2,1)S(1)} %fusion.11), channel_id=2, replica_groups=mesh['delay'=16,'row'=32] {'delay'}, dimensions={0}, use_global_device_ids=true | all-gather | bytes 278528 | tf_op jit(solution)/shard_map/all_gather | solution.py:31
  24.2 19.6 %all_to_all.30 = f32[32,2,256]{2,1,0:T(2,128)S(1)} all-to-all(f32[32,2,256]{2,1,0:T(2,128)S(1)} %copy.14), channel_id=1, replica_groups=mesh['delay'=16,'row'=32] {'row'}, dimensions={0} | all-to-all | bytes 131072 | tf_op jit(solution)/shard_map/all_to_all | solution.py:42
  45.1 4.0 %all-to-all-start.1 = ((bf16[32,2,256]{2,1,0:T(2,128)(2,1)}), bf16[32,2,256]{2,1,0:T(2,128)(2,1)S(1)}, u32[]{:S(2)}, u32[]{:S(2)}) async-start(bf16[32,2,256]{2,1,0:T(2,128)(2,1)} %broadcast_in_dim.22), calls=%async_computation.1 | async-start | bytes 65536 | tf_op jit(solution)/shard_map/all_to_all | solution.py:48
  49.1 3.5 %collective-permute-start = (f32[64,128]{1,0:T(8,128)S(1)}, f32[64,128]{1,0:T(8,128)S(1)}, u32[]{:S(2)}, u32[]{:S(2)}) collective-permute-start(f32[64,128]{1,0:T(8,128)S(1)} %bitcast.31), channel_id=1, source_target_pairs={{32,0},{64,32},{96,64},{128,96},{160,128},{192,160},{224,192},{256... | collective-permute-start | bytes 98312 | tf_op jit(solution)/shard_map/ppermute | solution.py:65
  52.9 4.9 %all-to-all-done.1 = bf16[32,2,256]{2,1,0:T(2,128)(2,1)S(1)} async-done(((bf16[32,2,256]{2,1,0:T(2,128)(2,1)}), bf16[32,2,256]{2,1,0:T(2,128)(2,1)S(1)}, u32[]{:S(2)}, u32[]{:S(2)}) %all-to-all-start.1) | async-done | bytes 32800 | tf_op jit(solution)/shard_map/all_to_all | solution.py:48
  57.7 2.5 collective-permute-start.1
  60.5 0.7 collective-permute-done.1
  61.2 2.3 collective-permute-start.3
  63.6 1.5 collective-permute-start.4
  65.0 0.7 collective-permute-done.3
  65.7 1.2 collective-permute-start.5
  66.9 2.7 %collective-permute-start.6 = (bf16[64,256]{1,0:T(8,128)(2,1)S(1)}, bf16[64,256]{1,0:T(8,128)(2,1)S(1)}, u32[]{:S(2)}, u32[]{:S(2)}) collective-permute-start(bf16[64,256]{1,0:T(8,128)(2,1)S(1)} %collective-permute-done.4), channel_id=1, source_target_pairs={{0,480},{32,0},{64,32},{96,64},{128,96},{160,128},{192,160},{224,1... | collective-permute-start | bytes 98312 | tf_op jit(solution)/shard_map/ppermute | solution.py:23
  69.6 0.7 collective-permute-done.5
  70.4 3.7 %collective-permute-start.8 = (bf16[64,256]{1,0:T(8,128)(2,1)S(1)}, bf16[64,256]{1,0:T(8,128)(2,1)S(1)}, u32[]{:S(2)}, u32[]{:S(2)}) collective-permute-start(bf16[64,256]{1,0:T(8,128)(2,1)S(1)} %collective-permute-done.6), channel_id=1, source_target_pairs={{0,480},{32,0},{64,32},{96,64},{128,96},{160,128},{192,160},{224,1... | collective-permute-start | bytes 98312 | tf_op jit(solution)/shard_map/ppermute | solution.py:23
  74.1 0.7 collective-permute-done.7
  75.0 3.7 %collective-permute-start.10 = (bf16[64,256]{1,0:T(8,128)(2,1)S(1)}, bf16[64,256]{1,0:T(8,128)(2,1)S(1)}, u32[]{:S(2)}, u32[]{:S(2)}) collective-permute-start(bf16[64,256]{1,0:T(8,128)(2,1)S(1)} %collective-permute-done.8), channel_id=1, source_target_pairs={{0,480},{32,0},{64,32},{96,64},{128,96},{160,128},{192,160},{224,1... | collective-permute-start | bytes 98312 | tf_op jit(solution)/shard_map/ppermute | solution.py:23
  78.7 0.7 collective-permute-done.9
  79.5 3.7 %collective-permute-start.12 = (bf16[64,256]{1,0:T(8,128)(2,1)S(1)}, bf16[64,256]{1,0:T(8,128)(2,1)S(1)}, u32[]{:S(2)}, u32[]{:S(2)}) collective-permute-start(bf16[64,256]{1,0:T(8,128)(2,1)S(1)} %collective-permute-done.10), channel_id=1, source_target_pairs={{0,480},{32,0},{64,32},{96,64},{128,96},{160,128},{192,160},{224,1... | collective-permute-start | bytes 98312 | tf_op jit(solution)/shard_map/ppermute | solution.py:23
  83.2 0.7 collective-permute-done.11
  84.1 3.7 %collective-permute-start.14 = (bf16[64,256]{1,0:T(8,128)(2,1)S(1)}, bf16[64,256]{1,0:T(8,128)(2,1)S(1)}, u32[]{:S(2)}, u32[]{:S(2)}) collective-permute-start(bf16[64,256]{1,0:T(8,128)(2,1)S(1)} %collective-permute-done.12), channel_id=1, source_target_pairs={{0,480},{32,0},{64,32},{96,64},{128,96},{160,128},{192,160},{224,1... | collective-permute-start | bytes 98312 | tf_op jit(solution)/shard_map/ppermute | solution.py:23
  87.8 0.7 collective-permute-done.13
  88.6 4.4 %collective-permute-done.15 = bf16[64,256]{1,0:T(8,128)(2,1)S(1)} collective-permute-done((bf16[64,256]{1,0:T(8,128)(2,1)S(1)}, bf16[64,256]{1,0:T(8,128)(2,1)S(1)}, u32[]{:S(2)}, u32[]{:S(2)}) %collective-permute-start.15) | collective-permute-done | bytes 32800 | tf_op jit(solution)/shard_map/ppermute | solution.py:18
  93.4 18.6 %all-gather.1 = bf16[1024,128]{1,0:T(8,128)(2,1)S(1)} all-gather(bf16[64,128]{1,0:T(8,128)(2,1)S(1)} %get-tuple-element.5), channel_id=3, replica_groups=mesh['delay'=16,'row'=32] {'delay'}, dimensions={0}, use_global_device_ids=true | all-gather | bytes 278528 | tf_op jit(solution)/shard_map/all_gather | solution.py:31
  112.1 11.8 %all_to_all.31 = f32[32,2,256]{2,1,0:T(2,128)S(1)} all-to-all(f32[32,2,256]{2,1,0:T(2,128)S(1)} %copy.16), channel_id=1, replica_groups=mesh['delay'=16,'row'=32] {'row'}, dimensions={0} | all-to-all | bytes 131072 | tf_op jit(solution)/shard_map/all_to_all | solution.py:42
  124.7 3.9 %all-to-all-start.3 = ((bf16[32,2,256]{2,1,0:T(2,128)(2,1)}), bf16[32,2,256]{2,1,0:T(2,128)(2,1)S(1)}, u32[]{:S(2)}, u32[]{:S(2)}) async-start(bf16[32,2,256]{2,1,0:T(2,128)(2,1)} %broadcast_in_dim.23), calls=%async_computation.3 | async-start | bytes 65536 | tf_op jit(solution)/shard_map/all_to_all | solution.py:48
  128.5 3.3 %collective-permute-start.16 = (f32[64,128]{1,0:T(8,128)S(1)}, f32[64,128]{1,0:T(8,128)S(1)}, u32[]{:S(2)}, u32[]{:S(2)}) collective-permute-start(f32[64,128]{1,0:T(8,128)S(1)} %get-tuple-element.6), channel_id=1, source_target_pairs={{32,0},{64,32},{96,64},{128,96},{160,128},{192,160},{224,192},{256... | collective-permute-start | bytes 98312 | tf_op jit(solution)/shard_map/ppermute | solution.py:65
  131.9 5.3 %all-to-all-done.3 = bf16[32,2,256]{2,1,0:T(2,128)(2,1)S(1)} async-done(((bf16[32,2,256]{2,1,0:T(2,128)(2,1)}), bf16[32,2,256]{2,1,0:T(2,128)(2,1)S(1)}, u32[]{:S(2)}, u32[]{:S(2)}) %all-to-all-start.3) | async-done | bytes 32800 | tf_op jit(solution)/shard_map/all_to_all | solution.py:48
  137.2 4.1 %collective-permute-start.17 = (bf16[64,256]{1,0:T(8,128)(2,1)S(1)}, bf16[64,256]{1,0:T(8,128)(2,1)S(1)}, u32[]{:S(2)}, u32[]{:S(2)}) collective-permute-start(bf16[64,256]{1,0:T(8,128)(2,1)S(1)} %reshape.27), channel_id=1, source_target_pairs={{0,32},{32,64},{64,96},{96,128},{128,160},{160,192},{192,224},{224... | collective-permute-start | bytes 98312 | tf_op jit(solution)/shard_map/ppermute | solution.py:18
  141.4 1.0 collective-permute-done.17
  142.4 2.3 collective-permute-start.19
  144.7 1.0 collective-permute-done.19
  145.7 2.3 collective-permute-start.21
  148.9 0.7 collective-permute-done.21
  149.5 1.8 collective-permute-start.23
  151.7 1.8 collective-permute-start.24
  153.4 0.7 collective-permute-done.23
  155.0 3.0 %collective-permute-start.26 = (bf16[64,256]{1,0:T(8,128)(2,1)S(1)}, bf16[64,256]{1,0:T(8,128)(2,1)S(1)}, u32[]{:S(2)}, u32[]{:S(2)}) collective-permute-start(bf16[64,256]{1,0:T(8,128)(2,1)S(1)} %collective-permute-done.24), channel_id=1, source_target_pairs={{0,480},{32,0},{64,32},{96,64},{128,96},{160,128},{192,160},{224,1... | collective-permute-start | bytes 98312 | tf_op jit(solution)/shard_map/ppermute | solution.py:23
  158.0 0.7 collective-permute-done.25
  158.8 3.7 %collective-permute-start.28 = (bf16[64,256]{1,0:T(8,128)(2,1)S(1)}, bf16[64,256]{1,0:T(8,128)(2,1)S(1)}, u32[]{:S(2)}, u32[]{:S(2)}) collective-permute-start(bf16[64,256]{1,0:T(8,128)(2,1)S(1)} %collective-permute-done.26), channel_id=1, source_target_pairs={{0,480},{32,0},{64,32},{96,64},{128,96},{160,128},{192,160},{224,1... | collective-permute-start | bytes 98312 | tf_op jit(solution)/shard_map/ppermute | solution.py:23
  162.5 0.7 collective-permute-done.27
  163.4 3.7 %collective-permute-start.30 = (bf16[64,256]{1,0:T(8,128)(2,1)S(1)}, bf16[64,256]{1,0:T(8,128)(2,1)S(1)}, u32[]{:S(2)}, u32[]{:S(2)}) collective-permute-start(bf16[64,256]{1,0:T(8,128)(2,1)S(1)} %collective-permute-done.28), channel_id=1, source_target_pairs={{0,480},{32,0},{64,32},{96,64},{128,96},{160,128},{192,160},{224,1... | collective-permute-start | bytes 98312 | tf_op jit(solution)/shard_map/ppermute | solution.py:23
  167.1 0.7 collective-permute-done.29
  168.0 4.4 %collective-permute-done.31 = bf16[64,256]{1,0:T(8,128)(2,1)S(1)} collective-permute-done((bf16[64,256]{1,0:T(8,128)(2,1)S(1)}, bf16[64,256]{1,0:T(8,128)(2,1)S(1)}, u32[]{:S(2)}, u32[]{:S(2)}) %collective-permute-start.31) | collective-permute-done | bytes 32800 | tf_op jit(solution)/shard_map/ppermute | solution.py:18
  172.7 18.6 %all-gather.2 = bf16[1024,128]{1,0:T(8,128)(2,1)S(1)} all-gather(bf16[64,128]{1,0:T(8,128)(2,1)S(1)} %get-tuple-element.7), channel_id=4, replica_groups=mesh['delay'=16,'row'=32] {'delay'}, dimensions={0}, use_global_device_ids=true | all-gather | bytes 278528 | tf_op jit(solution)/shard_map/all_gather | solution.py:31
  191.4 11.8 %all_to_all.32 = f32[32,2,256]{2,1,0:T(2,128)S(1)} all-to-all(f32[32,2,256]{2,1,0:T(2,128)S(1)} %copy.18), channel_id=1, replica_groups=mesh['delay'=16,'row'=32] {'row'}, dimensions={0} | all-to-all | bytes 131072 | tf_op jit(solution)/shard_map/all_to_all | solution.py:42
  203.9 3.9 %all-to-all-start.5 = ((bf16[32,2,256]{2,1,0:T(2,128)(2,1)}), bf16[32,2,256]{2,1,0:T(2,128)(2,1)S(1)}, u32[]{:S(2)}, u32[]{:S(2)}) async-start(bf16[32,2,256]{2,1,0:T(2,128)(2,1)} %broadcast_in_dim.24), calls=%async_computation.5 | async-start | bytes 65536 | tf_op jit(solution)/shard_map/all_to_all | solution.py:48
  207.9 3.3 %collective-permute-start.32 = (f32[64,128]{1,0:T(8,128)S(1)}, f32[64,128]{1,0:T(8,128)S(1)}, u32[]{:S(2)}, u32[]{:S(2)}) collective-permute-start(f32[64,128]{1,0:T(8,128)S(1)} %get-tuple-element.8), channel_id=1, source_target_pairs={{32,0},{64,32},{96,64},{128,96},{160,128},{192,160},{224,192},{256... | collective-permute-start | bytes 98312 | tf_op jit(solution)/shard_map/ppermute | solution.py:65
  211.2 5.3 %all-to-all-done.5 = bf16[32,2,256]{2,1,0:T(2,128)(2,1)S(1)} async-done(((bf16[32,2,256]{2,1,0:T(2,128)(2,1)}), bf16[32,2,256]{2,1,0:T(2,128)(2,1)S(1)}, u32[]{:S(2)}, u32[]{:S(2)}) %all-to-all-start.5) | async-done | bytes 32800 | tf_op jit(solution)/shard_map/all_to_all | solution.py:48
  216.5 4.1 %collective-permute-start.33 = (bf16[64,256]{1,0:T(8,128)(2,1)S(1)}, bf16[64,256]{1,0:T(8,128)(2,1)S(1)}, u32[]{:S(2)}, u32[]{:S(2)}) collective-permute-start(bf16[64,256]{1,0:T(8,128)(2,1)S(1)} %reshape.28), channel_id=1, source_target_pairs={{0,32},{32,64},{64,96},{96,128},{128,160},{160,192},{192,224},{224... | collective-permute-start | bytes 98312 | tf_op jit(solution)/shard_map/ppermute | solution.py:18
  221.6 2.3 collective-permute-start.35
  224.0 1.0 collective-permute-done.35
  225.0 2.3 collective-permute-start.37
  228.1 0.7 collective-permute-done.37
  228.8 1.8 collective-permute-start.39
  230.9 1.8 collective-permute-start.40
  234.3 3.0 %collective-permute-start.42 = (bf16[64,256]{1,0:T(8,128)(2,1)S(1)}, bf16[64,256]{1,0:T(8,128)(2,1)S(1)}, u32[]{:S(2)}, u32[]{:S(2)}) collective-permute-start(bf16[64,256]{1,0:T(8,128)(2,1)S(1)} %collective-permute-done.40), channel_id=1, source_target_pairs={{0,480},{32,0},{64,32},{96,64},{128,96},{160,128},{192,160},{224,1... | collective-permute-start | bytes 98312 | tf_op jit(solution)/shard_map/ppermute | solution.py:23
  237.2 0.7 collective-permute-done.41
  238.1 3.7 %collective-permute-start.44 = (bf16[64,256]{1,0:T(8,128)(2,1)S(1)}, bf16[64,256]{1,0:T(8,128)(2,1)S(1)}, u32[]{:S(2)}, u32[]{:S(2)}) collective-permute-start(bf16[64,256]{1,0:T(8,128)(2,1)S(1)} %collective-permute-done.42), channel_id=1, source_target_pairs={{0,480},{32,0},{64,32},{96,64},{128,96},{160,128},{192,160},{224,1... | collective-permute-start | bytes 98312 | tf_op jit(solution)/shard_map/ppermute | solution.py:23
  242.7 3.7 %collective-permute-start.46 = (bf16[64,256]{1,0:T(8,128)(2,1)S(1)}, bf16[64,256]{1,0:T(8,128)(2,1)S(1)}, u32[]{:S(2)}, u32[]{:S(2)}) collective-permute-start(bf16[64,256]{1,0:T(8,128)(2,1)S(1)} %collective-permute-done.44), channel_id=1, source_target_pairs={{0,480},{32,0},{64,32},{96,64},{128,96},{160,128},{192,160},{224,1... | collective-permute-start | bytes 98312 | tf_op jit(solution)/shard_map/ppermute | solution.py:23
  246.4 0.7 collective-permute-done.45
  247.2 4.4 %collective-permute-done.47 = bf16[64,256]{1,0:T(8,128)(2,1)S(1)} collective-permute-done((bf16[64,256]{1,0:T(8,128)(2,1)S(1)}, bf16[64,256]{1,0:T(8,128)(2,1)S(1)}, u32[]{:S(2)}, u32[]{:S(2)}) %collective-permute-start.47) | collective-permute-done | bytes 32800 | tf_op jit(solution)/shard_map/ppermute | solution.py:18
  251.6 0.9 fusion
  (135 shorter events, 13.1 us)
Async XLA Ops:
  0.6 92.4 %copy-start = (bf16[1,4096,128]{2,1,0:T(8,128)(2,1)S(1)}, bf16[1,4096,128]{2,1,0:T(8,128)(2,1)}, u32[]{:S(2)}) copy-start(bf16[1,4096,128]{2,1,0:T(8,128)(2,1)} %param.10) | copy-start | bytes 3145732
  2.3 21.7 %copy-start.1 = (bf16[128,256]{1,0:T(8,128)(2,1)S(1)}, bf16[128,256]{1,0:T(8,128)(2,1)}, u32[]{:S(2)}) copy-start(bf16[128,256]{1,0:T(8,128)(2,1)} %param.9) | copy-start | bytes 196612
  43.8 0.7 copy-start.4
  45.1 4.0 %copy-start.3 = (f32[1,64,128]{2,1,0:T(8,128)S(1)}, f32[1,64,128]{2,1,0:T(8,128)}, u32[]{:S(2)}) copy-start(f32[1,64,128]{2,1,0:T(8,128)} %param.11) | copy-start | bytes 98308
  45.1 12.6 %all-to-all-start.1 = ((bf16[32,2,256]{2,1,0:T(2,128)(2,1)}), bf16[32,2,256]{2,1,0:T(2,128)(2,1)S(1)}, u32[]{:S(2)}, u32[]{:S(2)}) async-start(bf16[32,2,256]{2,1,0:T(2,128)(2,1)} %broadcast_in_dim.22), calls=%async_computation.1 | async-start | bytes 65536 | tf_op jit(solution)/shard_map/all_to_all | solution.py:48
  49.1 43.9 %collective-permute-start = (f32[64,128]{1,0:T(8,128)S(1)}, f32[64,128]{1,0:T(8,128)S(1)}, u32[]{:S(2)}, u32[]{:S(2)}) collective-permute-start(f32[64,128]{1,0:T(8,128)S(1)} %bitcast.31), channel_id=1, source_target_pairs={{32,0},{64,32},{96,64},{128,96},{160,128},{192,160},{224,192},{256... | collective-permute-start | bytes 98312 | tf_op jit(solution)/shard_map/ppermute | solution.py:65
  57.7 3.5 %collective-permute-start.1 = (bf16[64,256]{1,0:T(8,128)(2,1)S(1)}, bf16[64,256]{1,0:T(8,128)(2,1)S(1)}, u32[]{:S(2)}, u32[]{:S(2)}) collective-permute-start(bf16[64,256]{1,0:T(8,128)(2,1)S(1)} %reshape.26), channel_id=1, source_target_pairs={{0,32},{32,64},{64,96},{96,128},{128,160},{160,192},{192,224},{224... | collective-permute-start | bytes 98312 | tf_op jit(solution)/shard_map/ppermute | solution.py:18
  60.2 3.3 %collective-permute-start.2 = (bf16[64,256]{1,0:T(8,128)(2,1)S(1)}, bf16[64,256]{1,0:T(8,128)(2,1)S(1)}, u32[]{:S(2)}, u32[]{:S(2)}) collective-permute-start(bf16[64,256]{1,0:T(8,128)(2,1)S(1)} %reshape.26), channel_id=1, source_target_pairs={{0,480},{32,0},{64,32},{96,64},{128,96},{160,128},{192,160},{224,1... | collective-permute-start | bytes 98312 | tf_op jit(solution)/shard_map/ppermute | solution.py:23
  61.2 4.5 %collective-permute-start.3 = (bf16[64,256]{1,0:T(8,128)(2,1)S(1)}, bf16[64,256]{1,0:T(8,128)(2,1)S(1)}, u32[]{:S(2)}, u32[]{:S(2)}) collective-permute-start(bf16[64,256]{1,0:T(8,128)(2,1)S(1)} %collective-permute-done.1), channel_id=1, source_target_pairs={{0,32},{32,64},{64,96},{96,128},{128,160},{160,192},{192,224},{224... | collective-permute-start | bytes 98312 | tf_op jit(solution)/shard_map/ppermute | solution.py:18
  63.6 3.3 %collective-permute-start.4 = (bf16[64,256]{1,0:T(8,128)(2,1)S(1)}, bf16[64,256]{1,0:T(8,128)(2,1)S(1)}, u32[]{:S(2)}, u32[]{:S(2)}) collective-permute-start(bf16[64,256]{1,0:T(8,128)(2,1)S(1)} %collective-permute-done.2), channel_id=1, source_target_pairs={{0,480},{32,0},{64,32},{96,64},{128,96},{160,128},{192,160},{224,1... | collective-permute-start | bytes 98312 | tf_op jit(solution)/shard_map/ppermute | solution.py:23
  65.7 4.6 %collective-permute-start.5 = (bf16[64,256]{1,0:T(8,128)(2,1)S(1)}, bf16[64,256]{1,0:T(8,128)(2,1)S(1)}, u32[]{:S(2)}, u32[]{:S(2)}) collective-permute-start(bf16[64,256]{1,0:T(8,128)(2,1)S(1)} %collective-permute-done.3), channel_id=1, source_target_pairs={{0,32},{32,64},{64,96},{96,128},{128,160},{160,192},{192,224},{224... | collective-permute-start | bytes 98312 | tf_op jit(solution)/shard_map/ppermute | solution.py:18
  66.9 3.5 %collective-permute-start.6 = (bf16[64,256]{1,0:T(8,128)(2,1)S(1)}, bf16[64,256]{1,0:T(8,128)(2,1)S(1)}, u32[]{:S(2)}, u32[]{:S(2)}) collective-permute-start(bf16[64,256]{1,0:T(8,128)(2,1)S(1)} %collective-permute-done.4), channel_id=1, source_target_pairs={{0,480},{32,0},{64,32},{96,64},{128,96},{160,128},{192,160},{224,1... | collective-permute-start | bytes 98312 | tf_op jit(solution)/shard_map/ppermute | solution.py:23
  70.3 4.6 %collective-permute-start.7 = (bf16[64,256]{1,0:T(8,128)(2,1)S(1)}, bf16[64,256]{1,0:T(8,128)(2,1)S(1)}, u32[]{:S(2)}, u32[]{:S(2)}) collective-permute-start(bf16[64,256]{1,0:T(8,128)(2,1)S(1)} %collective-permute-done.5), channel_id=1, source_target_pairs={{0,32},{32,64},{64,96},{96,128},{128,160},{160,192},{192,224},{224... | collective-permute-start | bytes 98312 | tf_op jit(solution)/shard_map/ppermute | solution.py:18
  70.4 4.6 %collective-permute-start.8 = (bf16[64,256]{1,0:T(8,128)(2,1)S(1)}, bf16[64,256]{1,0:T(8,128)(2,1)S(1)}, u32[]{:S(2)}, u32[]{:S(2)}) collective-permute-start(bf16[64,256]{1,0:T(8,128)(2,1)S(1)} %collective-permute-done.6), channel_id=1, source_target_pairs={{0,480},{32,0},{64,32},{96,64},{128,96},{160,128},{192,160},{224,1... | collective-permute-start | bytes 98312 | tf_op jit(solution)/shard_map/ppermute | solution.py:23
  74.8 4.6 %collective-permute-start.9 = (bf16[64,256]{1,0:T(8,128)(2,1)S(1)}, bf16[64,256]{1,0:T(8,128)(2,1)S(1)}, u32[]{:S(2)}, u32[]{:S(2)}) collective-permute-start(bf16[64,256]{1,0:T(8,128)(2,1)S(1)} %collective-permute-done.7), channel_id=1, source_target_pairs={{0,32},{32,64},{64,96},{96,128},{128,160},{160,192},{192,224},{224... | collective-permute-start | bytes 98312 | tf_op jit(solution)/shard_map/ppermute | solution.py:18
  75.0 4.6 %collective-permute-start.10 = (bf16[64,256]{1,0:T(8,128)(2,1)S(1)}, bf16[64,256]{1,0:T(8,128)(2,1)S(1)}, u32[]{:S(2)}, u32[]{:S(2)}) collective-permute-start(bf16[64,256]{1,0:T(8,128)(2,1)S(1)} %collective-permute-done.8), channel_id=1, source_target_pairs={{0,480},{32,0},{64,32},{96,64},{128,96},{160,128},{192,160},{224,1... | collective-permute-start | bytes 98312 | tf_op jit(solution)/shard_map/ppermute | solution.py:23
  79.4 4.6 %collective-permute-start.11 = (bf16[64,256]{1,0:T(8,128)(2,1)S(1)}, bf16[64,256]{1,0:T(8,128)(2,1)S(1)}, u32[]{:S(2)}, u32[]{:S(2)}) collective-permute-start(bf16[64,256]{1,0:T(8,128)(2,1)S(1)} %collective-permute-done.9), channel_id=1, source_target_pairs={{0,32},{32,64},{64,96},{96,128},{128,160},{160,192},{192,224},{224... | collective-permute-start | bytes 98312 | tf_op jit(solution)/shard_map/ppermute | solution.py:18
  79.5 4.6 %collective-permute-start.12 = (bf16[64,256]{1,0:T(8,128)(2,1)S(1)}, bf16[64,256]{1,0:T(8,128)(2,1)S(1)}, u32[]{:S(2)}, u32[]{:S(2)}) collective-permute-start(bf16[64,256]{1,0:T(8,128)(2,1)S(1)} %collective-permute-done.10), channel_id=1, source_target_pairs={{0,480},{32,0},{64,32},{96,64},{128,96},{160,128},{192,160},{224,1... | collective-permute-start | bytes 98312 | tf_op jit(solution)/shard_map/ppermute | solution.py:23
  83.9 4.6 %collective-permute-start.13 = (bf16[64,256]{1,0:T(8,128)(2,1)S(1)}, bf16[64,256]{1,0:T(8,128)(2,1)S(1)}, u32[]{:S(2)}, u32[]{:S(2)}) collective-permute-start(bf16[64,256]{1,0:T(8,128)(2,1)S(1)} %collective-permute-done.11), channel_id=1, source_target_pairs={{0,32},{32,64},{64,96},{96,128},{128,160},{160,192},{192,224},{224... | collective-permute-start | bytes 98312 | tf_op jit(solution)/shard_map/ppermute | solution.py:18
  84.1 4.6 %collective-permute-start.14 = (bf16[64,256]{1,0:T(8,128)(2,1)S(1)}, bf16[64,256]{1,0:T(8,128)(2,1)S(1)}, u32[]{:S(2)}, u32[]{:S(2)}) collective-permute-start(bf16[64,256]{1,0:T(8,128)(2,1)S(1)} %collective-permute-done.12), channel_id=1, source_target_pairs={{0,480},{32,0},{64,32},{96,64},{128,96},{160,128},{192,160},{224,1... | collective-permute-start | bytes 98312 | tf_op jit(solution)/shard_map/ppermute | solution.py:23
  88.5 4.6 %collective-permute-start.15 = (bf16[64,256]{1,0:T(8,128)(2,1)S(1)}, bf16[64,256]{1,0:T(8,128)(2,1)S(1)}, u32[]{:S(2)}, u32[]{:S(2)}) collective-permute-start(bf16[64,256]{1,0:T(8,128)(2,1)S(1)} %collective-permute-done.13), channel_id=1, source_target_pairs={{0,32},{32,64},{64,96},{96,128},{128,160},{160,192},{192,224},{224... | collective-permute-start | bytes 98312 | tf_op jit(solution)/shard_map/ppermute | solution.py:18
  88.6 4.4 %copy-start.2 = (bf16[64,128]{1,0:T(8,128)(2,1)S(1)}, bf16[64,128]{1,0:T(8,128)(2,1)}, u32[]{:S(2)}) copy-start(bf16[64,128]{1,0:T(8,128)(2,1)} %param.6) | copy-start | bytes 49156
  124.7 12.5 %all-to-all-start.3 = ((bf16[32,2,256]{2,1,0:T(2,128)(2,1)}), bf16[32,2,256]{2,1,0:T(2,128)(2,1)S(1)}, u32[]{:S(2)}, u32[]{:S(2)}) async-start(bf16[32,2,256]{2,1,0:T(2,128)(2,1)} %broadcast_in_dim.23), calls=%async_computation.3 | async-start | bytes 65536 | tf_op jit(solution)/shard_map/all_to_all | solution.py:48
  128.5 43.8 %collective-permute-start.16 = (f32[64,128]{1,0:T(8,128)S(1)}, f32[64,128]{1,0:T(8,128)S(1)}, u32[]{:S(2)}, u32[]{:S(2)}) collective-permute-start(f32[64,128]{1,0:T(8,128)S(1)} %get-tuple-element.6), channel_id=1, source_target_pairs={{32,0},{64,32},{96,64},{128,96},{160,128},{192,160},{224,192},{256... | collective-permute-start | bytes 98312 | tf_op jit(solution)/shard_map/ppermute | solution.py:65
  137.2 5.2 %collective-permute-start.17 = (bf16[64,256]{1,0:T(8,128)(2,1)S(1)}, bf16[64,256]{1,0:T(8,128)(2,1)S(1)}, u32[]{:S(2)}, u32[]{:S(2)}) collective-permute-start(bf16[64,256]{1,0:T(8,128)(2,1)S(1)} %reshape.27), channel_id=1, source_target_pairs={{0,32},{32,64},{64,96},{96,128},{128,160},{160,192},{192,224},{224... | collective-permute-start | bytes 98312 | tf_op jit(solution)/shard_map/ppermute | solution.py:18
  141.3 3.3 %collective-permute-start.18 = (bf16[64,256]{1,0:T(8,128)(2,1)S(1)}, bf16[64,256]{1,0:T(8,128)(2,1)S(1)}, u32[]{:S(2)}, u32[]{:S(2)}) collective-permute-start(bf16[64,256]{1,0:T(8,128)(2,1)S(1)} %reshape.27), channel_id=1, source_target_pairs={{0,480},{32,0},{64,32},{96,64},{128,96},{160,128},{192,160},{224,1... | collective-permute-start | bytes 98312 | tf_op jit(solution)/shard_map/ppermute | solution.py:23
  142.4 3.3 %collective-permute-start.19 = (bf16[64,256]{1,0:T(8,128)(2,1)S(1)}, bf16[64,256]{1,0:T(8,128)(2,1)S(1)}, u32[]{:S(2)}, u32[]{:S(2)}) collective-permute-start(bf16[64,256]{1,0:T(8,128)(2,1)S(1)} %collective-permute-done.17), channel_id=1, source_target_pairs={{0,32},{32,64},{64,96},{96,128},{128,160},{160,192},{192,224},{224... | collective-permute-start | bytes 98312 | tf_op jit(solution)/shard_map/ppermute | solution.py:18
  144.7 3.6 %collective-permute-start.20 = (bf16[64,256]{1,0:T(8,128)(2,1)S(1)}, bf16[64,256]{1,0:T(8,128)(2,1)S(1)}, u32[]{:S(2)}, u32[]{:S(2)}) collective-permute-start(bf16[64,256]{1,0:T(8,128)(2,1)S(1)} %collective-permute-done.18), channel_id=1, source_target_pairs={{0,480},{32,0},{64,32},{96,64},{128,96},{160,128},{192,160},{224,1... | collective-permute-start | bytes 98312 | tf_op jit(solution)/shard_map/ppermute | solution.py:23
  145.7 3.8 %collective-permute-start.21 = (bf16[64,256]{1,0:T(8,128)(2,1)S(1)}, bf16[64,256]{1,0:T(8,128)(2,1)S(1)}, u32[]{:S(2)}, u32[]{:S(2)}) collective-permute-start(bf16[64,256]{1,0:T(8,128)(2,1)S(1)} %collective-permute-done.19), channel_id=1, source_target_pairs={{0,32},{32,64},{64,96},{96,128},{128,160},{160,192},{192,224},{224... | collective-permute-start | bytes 98312 | tf_op jit(solution)/shard_map/ppermute | solution.py:18
  148.3 3.3 %collective-permute-start.22 = (bf16[64,256]{1,0:T(8,128)(2,1)S(1)}, bf16[64,256]{1,0:T(8,128)(2,1)S(1)}, u32[]{:S(2)}, u32[]{:S(2)}) collective-permute-start(bf16[64,256]{1,0:T(8,128)(2,1)S(1)} %collective-permute-done.20), channel_id=1, source_target_pairs={{0,480},{32,0},{64,32},{96,64},{128,96},{160,128},{192,160},{224,1... | collective-permute-start | bytes 98312 | tf_op jit(solution)/shard_map/ppermute | solution.py:23
  149.5 4.6 %collective-permute-start.23 = (bf16[64,256]{1,0:T(8,128)(2,1)S(1)}, bf16[64,256]{1,0:T(8,128)(2,1)S(1)}, u32[]{:S(2)}, u32[]{:S(2)}) collective-permute-start(bf16[64,256]{1,0:T(8,128)(2,1)S(1)} %collective-permute-done.21), channel_id=1, source_target_pairs={{0,32},{32,64},{64,96},{96,128},{128,160},{160,192},{192,224},{224... | collective-permute-start | bytes 98312 | tf_op jit(solution)/shard_map/ppermute | solution.py:18
  151.7 3.3 %collective-permute-start.24 = (bf16[64,256]{1,0:T(8,128)(2,1)S(1)}, bf16[64,256]{1,0:T(8,128)(2,1)S(1)}, u32[]{:S(2)}, u32[]{:S(2)}) collective-permute-start(bf16[64,256]{1,0:T(8,128)(2,1)S(1)} %collective-permute-done.22), channel_id=1, source_target_pairs={{0,480},{32,0},{64,32},{96,64},{128,96},{160,128},{192,160},{224,1... | collective-permute-start | bytes 98312 | tf_op jit(solution)/shard_map/ppermute | solution.py:23
  154.1 4.6 %collective-permute-start.25 = (bf16[64,256]{1,0:T(8,128)(2,1)S(1)}, bf16[64,256]{1,0:T(8,128)(2,1)S(1)}, u32[]{:S(2)}, u32[]{:S(2)}) collective-permute-start(bf16[64,256]{1,0:T(8,128)(2,1)S(1)} %collective-permute-done.23), channel_id=1, source_target_pairs={{0,32},{32,64},{64,96},{96,128},{128,160},{160,192},{192,224},{224... | collective-permute-start | bytes 98312 | tf_op jit(solution)/shard_map/ppermute | solution.py:18
  155.0 3.8 %collective-permute-start.26 = (bf16[64,256]{1,0:T(8,128)(2,1)S(1)}, bf16[64,256]{1,0:T(8,128)(2,1)S(1)}, u32[]{:S(2)}, u32[]{:S(2)}) collective-permute-start(bf16[64,256]{1,0:T(8,128)(2,1)S(1)} %collective-permute-done.24), channel_id=1, source_target_pairs={{0,480},{32,0},{64,32},{96,64},{128,96},{160,128},{192,160},{224,1... | collective-permute-start | bytes 98312 | tf_op jit(solution)/shard_map/ppermute | solution.py:23
  158.7 4.6 %collective-permute-start.27 = (bf16[64,256]{1,0:T(8,128)(2,1)S(1)}, bf16[64,256]{1,0:T(8,128)(2,1)S(1)}, u32[]{:S(2)}, u32[]{:S(2)}) collective-permute-start(bf16[64,256]{1,0:T(8,128)(2,1)S(1)} %collective-permute-done.25), channel_id=1, source_target_pairs={{0,32},{32,64},{64,96},{96,128},{128,160},{160,192},{192,224},{224... | collective-permute-start | bytes 98312 | tf_op jit(solution)/shard_map/ppermute | solution.py:18
  158.8 4.6 %collective-permute-start.28 = (bf16[64,256]{1,0:T(8,128)(2,1)S(1)}, bf16[64,256]{1,0:T(8,128)(2,1)S(1)}, u32[]{:S(2)}, u32[]{:S(2)}) collective-permute-start(bf16[64,256]{1,0:T(8,128)(2,1)S(1)} %collective-permute-done.26), channel_id=1, source_target_pairs={{0,480},{32,0},{64,32},{96,64},{128,96},{160,128},{192,160},{224,1... | collective-permute-start | bytes 98312 | tf_op jit(solution)/shard_map/ppermute | solution.py:23
  163.2 4.6 %collective-permute-start.29 = (bf16[64,256]{1,0:T(8,128)(2,1)S(1)}, bf16[64,256]{1,0:T(8,128)(2,1)S(1)}, u32[]{:S(2)}, u32[]{:S(2)}) collective-permute-start(bf16[64,256]{1,0:T(8,128)(2,1)S(1)} %collective-permute-done.27), channel_id=1, source_target_pairs={{0,32},{32,64},{64,96},{96,128},{128,160},{160,192},{192,224},{224... | collective-permute-start | bytes 98312 | tf_op jit(solution)/shard_map/ppermute | solution.py:18
  163.4 4.6 %collective-permute-start.30 = (bf16[64,256]{1,0:T(8,128)(2,1)S(1)}, bf16[64,256]{1,0:T(8,128)(2,1)S(1)}, u32[]{:S(2)}, u32[]{:S(2)}) collective-permute-start(bf16[64,256]{1,0:T(8,128)(2,1)S(1)} %collective-permute-done.28), channel_id=1, source_target_pairs={{0,480},{32,0},{64,32},{96,64},{128,96},{160,128},{192,160},{224,1... | collective-permute-start | bytes 98312 | tf_op jit(solution)/shard_map/ppermute | solution.py:23
  167.8 4.6 %collective-permute-start.31 = (bf16[64,256]{1,0:T(8,128)(2,1)S(1)}, bf16[64,256]{1,0:T(8,128)(2,1)S(1)}, u32[]{:S(2)}, u32[]{:S(2)}) collective-permute-start(bf16[64,256]{1,0:T(8,128)(2,1)S(1)} %collective-permute-done.29), channel_id=1, source_target_pairs={{0,32},{32,64},{64,96},{96,128},{128,160},{160,192},{192,224},{224... | collective-permute-start | bytes 98312 | tf_op jit(solution)/shard_map/ppermute | solution.py:18
  203.9 12.5 %all-to-all-start.5 = ((bf16[32,2,256]{2,1,0:T(2,128)(2,1)}), bf16[32,2,256]{2,1,0:T(2,128)(2,1)S(1)}, u32[]{:S(2)}, u32[]{:S(2)}) async-start(bf16[32,2,256]{2,1,0:T(2,128)(2,1)} %broadcast_in_dim.24), calls=%async_computation.5 | async-start | bytes 65536 | tf_op jit(solution)/shard_map/all_to_all | solution.py:48
  207.9 43.7 %collective-permute-start.32 = (f32[64,128]{1,0:T(8,128)S(1)}, f32[64,128]{1,0:T(8,128)S(1)}, u32[]{:S(2)}, u32[]{:S(2)}) collective-permute-start(f32[64,128]{1,0:T(8,128)S(1)} %get-tuple-element.8), channel_id=1, source_target_pairs={{32,0},{64,32},{96,64},{128,96},{160,128},{192,160},{224,192},{256... | collective-permute-start | bytes 98312 | tf_op jit(solution)/shard_map/ppermute | solution.py:65
  216.5 5.2 %collective-permute-start.33 = (bf16[64,256]{1,0:T(8,128)(2,1)S(1)}, bf16[64,256]{1,0:T(8,128)(2,1)S(1)}, u32[]{:S(2)}, u32[]{:S(2)}) collective-permute-start(bf16[64,256]{1,0:T(8,128)(2,1)S(1)} %reshape.28), channel_id=1, source_target_pairs={{0,32},{32,64},{64,96},{96,128},{128,160},{160,192},{192,224},{224... | collective-permute-start | bytes 98312 | tf_op jit(solution)/shard_map/ppermute | solution.py:18
  220.6 3.3 %collective-permute-start.34 = (bf16[64,256]{1,0:T(8,128)(2,1)S(1)}, bf16[64,256]{1,0:T(8,128)(2,1)S(1)}, u32[]{:S(2)}, u32[]{:S(2)}) collective-permute-start(bf16[64,256]{1,0:T(8,128)(2,1)S(1)} %reshape.28), channel_id=1, source_target_pairs={{0,480},{32,0},{64,32},{96,64},{128,96},{160,128},{192,160},{224,1... | collective-permute-start | bytes 98312 | tf_op jit(solution)/shard_map/ppermute | solution.py:23
  221.6 3.3 %collective-permute-start.35 = (bf16[64,256]{1,0:T(8,128)(2,1)S(1)}, bf16[64,256]{1,0:T(8,128)(2,1)S(1)}, u32[]{:S(2)}, u32[]{:S(2)}) collective-permute-start(bf16[64,256]{1,0:T(8,128)(2,1)S(1)} %collective-permute-done.33), channel_id=1, source_target_pairs={{0,32},{32,64},{64,96},{96,128},{128,160},{160,192},{192,224},{224... | collective-permute-start | bytes 98312 | tf_op jit(solution)/shard_map/ppermute | solution.py:18
  223.9 3.6 %collective-permute-start.36 = (bf16[64,256]{1,0:T(8,128)(2,1)S(1)}, bf16[64,256]{1,0:T(8,128)(2,1)S(1)}, u32[]{:S(2)}, u32[]{:S(2)}) collective-permute-start(bf16[64,256]{1,0:T(8,128)(2,1)S(1)} %collective-permute-done.34), channel_id=1, source_target_pairs={{0,480},{32,0},{64,32},{96,64},{128,96},{160,128},{192,160},{224,1... | collective-permute-start | bytes 98312 | tf_op jit(solution)/shard_map/ppermute | solution.py:23
  225.0 3.8 %collective-permute-start.37 = (bf16[64,256]{1,0:T(8,128)(2,1)S(1)}, bf16[64,256]{1,0:T(8,128)(2,1)S(1)}, u32[]{:S(2)}, u32[]{:S(2)}) collective-permute-start(bf16[64,256]{1,0:T(8,128)(2,1)S(1)} %collective-permute-done.35), channel_id=1, source_target_pairs={{0,32},{32,64},{64,96},{96,128},{128,160},{160,192},{192,224},{224... | collective-permute-start | bytes 98312 | tf_op jit(solution)/shard_map/ppermute | solution.py:18
  227.6 3.3 %collective-permute-start.38 = (bf16[64,256]{1,0:T(8,128)(2,1)S(1)}, bf16[64,256]{1,0:T(8,128)(2,1)S(1)}, u32[]{:S(2)}, u32[]{:S(2)}) collective-permute-start(bf16[64,256]{1,0:T(8,128)(2,1)S(1)} %collective-permute-done.36), channel_id=1, source_target_pairs={{0,480},{32,0},{64,32},{96,64},{128,96},{160,128},{192,160},{224,1... | collective-permute-start | bytes 98312 | tf_op jit(solution)/shard_map/ppermute | solution.py:23
  228.8 4.6 %collective-permute-start.39 = (bf16[64,256]{1,0:T(8,128)(2,1)S(1)}, bf16[64,256]{1,0:T(8,128)(2,1)S(1)}, u32[]{:S(2)}, u32[]{:S(2)}) collective-permute-start(bf16[64,256]{1,0:T(8,128)(2,1)S(1)} %collective-permute-done.37), channel_id=1, source_target_pairs={{0,32},{32,64},{64,96},{96,128},{128,160},{160,192},{192,224},{224... | collective-permute-start | bytes 98312 | tf_op jit(solution)/shard_map/ppermute | solution.py:18
  230.9 3.3 %collective-permute-start.40 = (bf16[64,256]{1,0:T(8,128)(2,1)S(1)}, bf16[64,256]{1,0:T(8,128)(2,1)S(1)}, u32[]{:S(2)}, u32[]{:S(2)}) collective-permute-start(bf16[64,256]{1,0:T(8,128)(2,1)S(1)} %collective-permute-done.38), channel_id=1, source_target_pairs={{0,480},{32,0},{64,32},{96,64},{128,96},{160,128},{192,160},{224,1... | collective-permute-start | bytes 98312 | tf_op jit(solution)/shard_map/ppermute | solution.py:23
  233.4 4.6 %collective-permute-start.41 = (bf16[64,256]{1,0:T(8,128)(2,1)S(1)}, bf16[64,256]{1,0:T(8,128)(2,1)S(1)}, u32[]{:S(2)}, u32[]{:S(2)}) collective-permute-start(bf16[64,256]{1,0:T(8,128)(2,1)S(1)} %collective-permute-done.39), channel_id=1, source_target_pairs={{0,32},{32,64},{64,96},{96,128},{128,160},{160,192},{192,224},{224... | collective-permute-start | bytes 98312 | tf_op jit(solution)/shard_map/ppermute | solution.py:18
  234.3 3.8 %collective-permute-start.42 = (bf16[64,256]{1,0:T(8,128)(2,1)S(1)}, bf16[64,256]{1,0:T(8,128)(2,1)S(1)}, u32[]{:S(2)}, u32[]{:S(2)}) collective-permute-start(bf16[64,256]{1,0:T(8,128)(2,1)S(1)} %collective-permute-done.40), channel_id=1, source_target_pairs={{0,480},{32,0},{64,32},{96,64},{128,96},{160,128},{192,160},{224,1... | collective-permute-start | bytes 98312 | tf_op jit(solution)/shard_map/ppermute | solution.py:23
  237.9 4.6 %collective-permute-start.43 = (bf16[64,256]{1,0:T(8,128)(2,1)S(1)}, bf16[64,256]{1,0:T(8,128)(2,1)S(1)}, u32[]{:S(2)}, u32[]{:S(2)}) collective-permute-start(bf16[64,256]{1,0:T(8,128)(2,1)S(1)} %collective-permute-done.41), channel_id=1, source_target_pairs={{0,32},{32,64},{64,96},{96,128},{128,160},{160,192},{192,224},{224... | collective-permute-start | bytes 98312 | tf_op jit(solution)/shard_map/ppermute | solution.py:18
  238.1 4.6 %collective-permute-start.44 = (bf16[64,256]{1,0:T(8,128)(2,1)S(1)}, bf16[64,256]{1,0:T(8,128)(2,1)S(1)}, u32[]{:S(2)}, u32[]{:S(2)}) collective-permute-start(bf16[64,256]{1,0:T(8,128)(2,1)S(1)} %collective-permute-done.42), channel_id=1, source_target_pairs={{0,480},{32,0},{64,32},{96,64},{128,96},{160,128},{192,160},{224,1... | collective-permute-start | bytes 98312 | tf_op jit(solution)/shard_map/ppermute | solution.py:23
  242.5 4.6 %collective-permute-start.45 = (bf16[64,256]{1,0:T(8,128)(2,1)S(1)}, bf16[64,256]{1,0:T(8,128)(2,1)S(1)}, u32[]{:S(2)}, u32[]{:S(2)}) collective-permute-start(bf16[64,256]{1,0:T(8,128)(2,1)S(1)} %collective-permute-done.43), channel_id=1, source_target_pairs={{0,32},{32,64},{64,96},{96,128},{128,160},{160,192},{192,224},{224... | collective-permute-start | bytes 98312 | tf_op jit(solution)/shard_map/ppermute | solution.py:18
  242.7 4.6 %collective-permute-start.46 = (bf16[64,256]{1,0:T(8,128)(2,1)S(1)}, bf16[64,256]{1,0:T(8,128)(2,1)S(1)}, u32[]{:S(2)}, u32[]{:S(2)}) collective-permute-start(bf16[64,256]{1,0:T(8,128)(2,1)S(1)} %collective-permute-done.44), channel_id=1, source_target_pairs={{0,480},{32,0},{64,32},{96,64},{128,96},{160,128},{192,160},{224,1... | collective-permute-start | bytes 98312 | tf_op jit(solution)/shard_map/ppermute | solution.py:23
  247.0 4.6 %collective-permute-start.47 = (bf16[64,256]{1,0:T(8,128)(2,1)S(1)}, bf16[64,256]{1,0:T(8,128)(2,1)S(1)}, u32[]{:S(2)}, u32[]{:S(2)}) collective-permute-start(bf16[64,256]{1,0:T(8,128)(2,1)S(1)} %collective-permute-done.45), channel_id=1, source_target_pairs={{0,32},{32,64},{64,96},{96,128},{128,160},{160,192},{192,224},{224... | collective-permute-start | bytes 98312 | tf_op jit(solution)/shard_map/ppermute | solution.py:18
